TPU v7x, 512 devices: a whole 4x4x16 slice. The times are simulated.
512 devices in a mesh: dp: 8 (over z_hi, core), mp: 64 (over y, z_lo, x).
Axes of the slice: x: 4, y: 4, z: 16 (z_hi: 4, z_lo: 4; z = z_hi * 4 + z_lo), core: 2. Of those that a mesh axis runs over, the one named last changes fastest.
Arguments:
- tokens: bfloat16 [65536, 4096], P(('dp', 'mp')), may hold values from -6 to 6
- grad_out: bfloat16 [14336, 65536], P('mp', 'dp'), may hold values from -0.0234375 to 0.0234375
- basis: bfloat16 [4096, 512], P('mp'), may hold values from -0.09375 to 0.09375
- first_in: float32 [14336, 512], P('mp', 'dp'), may hold values from -6 to 6
- second_in: float32 [14336, 512], P('mp', 'dp'), may hold values from 0.005 to 0.05
Outputs:
- update: bfloat16 [14336, 4096], P('mp', 'dp')
- first_moment: float32 [14336, 512], P('mp', 'dp')
- second_moment: float32 [14336, 512], P('mp', 'dp')
All inputs are finite; a program needn't handle non-finite values.
Results may differ from a plain program's by a relative error of at most 0.0049.
Values may be sent and summed in bfloat16 or wider, within the bound.
A program may use at most 64 MiB of HBM per device.

v0:
```python
import jax
import jax.numpy as jnp
from jax import lax
from jax.sharding import PartitionSpec as P

STEP = 10


beta_one = 0.9
beta_two = 0.999
epsilon = 1e-08


def adam_step(gradient, first_old, second_old):
    first_new = beta_one * first_old + (1.0 - beta_one) * gradient
    second_new = beta_two * second_old + (1.0 - beta_two) * gradient * gradient
    corr_one = 1.0 - beta_one**STEP
    corr_two = 1.0 - beta_two**STEP
    direction = (first_new / corr_one / (jnp.sqrt(second_new / corr_two) + epsilon)).astype(
        jnp.bfloat16
    )
    return (first_new, second_new, direction)


def per_device(tokens, grad_out, basis, first_in, second_in):
    whole_basis = lax.all_gather(basis, "mp", axis=0, tiled=True)
    projected = jnp.dot(tokens, whole_basis, preferred_element_type=jnp.float32).astype(
        jnp.bfloat16
    )
    gathered = lax.all_gather(projected, "mp", axis=0, tiled=True)
    partial_grad = jnp.dot(grad_out, gathered, preferred_element_type=jnp.float32)
    groups = lax.axis_size("dp")
    group_index = lax.axis_index("dp")
    state_count = first_in.shape[1]
    row_count = whole_basis.shape[0] // groups
    basis_block = lax.dynamic_slice_in_dim(whole_basis, group_index * row_count, row_count, 0)
    total_grad = lax.psum(partial_grad, "dp")
    own_grad = lax.dynamic_slice_in_dim(total_grad, group_index * state_count, state_count, 1)
    first_moment, second_moment, direction = adam_step(own_grad, first_in, second_in)
    full_direction = lax.all_gather(direction, "dp", axis=1, tiled=True)
    update = lax.dot_general(
        full_direction, basis_block, (((1,), (1,)), ((), ())), preferred_element_type=jnp.float32
    ).astype(jnp.bfloat16)
    return (update, first_moment, second_moment)


def solution(mesh):
    in_specs = (P(("dp", "mp"), None), P("mp", "dp"), P("mp", None), P("mp", "dp"), P("mp", "dp"))
    out_specs = (P("mp", "dp"), P("mp", "dp"), P("mp", "dp"))
    return jax.shard_map(
        per_device, mesh=mesh, in_specs=in_specs, out_specs=out_specs, check_vma=False
    )
```

profile of v0, /device:TPU:1, one launch (start us, length us, event | category | flops | bytes accessed | tf_op | source)
XLA Modules:
  0.0 877.5 jit_solution(172996368841249202)
XLA Ops:
  7.2 0.0 copy-start
  7.2 0.0 all-gather.3.cloned.1.call-start
  7.2 0.7 all-gather.3.cloned.1.call-update
  7.9 0.0 all-gather.5.cloned.1.call-start
  8.0 325.0 %all-gather.3.cloned.1.call-done = bf16[4096,512]{1,0:T(8,128)(2,1)} async-done(((bf16[64,512]{1,0:T(8,128)(2,1)}), bf16[4096,512]{1,0:T(8,128)(2,1)}) %all-gather.3.cloned.1.call-update) | async-done | bytes 4194320 | tf_op jit(solution)/shard_map/all_gather | solution.py:26
  332.9 0.0 copy-done
  332.9 3.6 convolution_convert_fusion.1
  336.5 0.0 all-gather.5.cloned.1.call-update
  336.5 0.0 copy-start.1
  336.5 0.0 copy-start.2
  336.5 0.0 all-reduce.2.cloned.1.call-start
  336.6 365.3 %all-gather.5.cloned.1.call-done = bf16[8192,512]{1,0:T(8,128)(2,1)} async-done(((bf16[128,512]{1,0:T(8,128)(2,1)}), bf16[8192,512]{1,0:T(8,128)(2,1)}) %all-gather.5.cloned.1.call-update) | async-done | bytes 8388624 | tf_op jit(solution)/shard_map/all_gather | solution.py:30
  701.9 7.6 convolution_bitcast_fusion
  709.5 0.0 all-reduce.2.cloned.1.call-update
  709.5 138.4 %all-reduce.2.cloned.1.call-done = f32[224,512]{0,1:T(8,128)} async-done(((f32[224,512]{0,1:T(8,128)}), f32[224,512]{0,1:T(8,128)}) %all-reduce.2.cloned.1.call-update) | async-done | bytes 458768 | tf_op jit(solution)/shard_map/psum | solution.py:37
  847.9 0.0 copy-done.1
  847.9 0.0 copy-done.2
  847.9 1.5 divide_convert_fusion
  849.5 19.5 %all_gather.11 = bf16[224,512]{0,1:T(8,128)(2,1)S(1)} all-gather(bf16[224,64]{0,1:T(8,128)(2,1)S(1)} %get-tuple-element.9), channel_id=1, replica_groups=mesh['dp'=8,'mp'=64] {'dp'}, dimensions={1}, use_global_device_ids=true | all-gather | bytes 258048 | tf_op jit(solution)/shard_map/all_gather | solution.py:40
  868.9 2.1 convolution_convert_fusion
Async XLA Ops:
  7.2 325.8 %copy-start = (bf16[128,4096]{1,0:T(8,128)(2,1)S(1)}, bf16[128,4096]{1,0:T(8,128)(2,1)}, u32[]{:S(2)}) copy-start(bf16[128,4096]{1,0:T(8,128)(2,1)} %param.5) | copy-start | bytes 3145732
  7.2 325.7 %all-gather.3.cloned.1.call-start = ((), (), s32[]{:S(2)}) async-start(), calls=%async_computation | async-start | bytes 4259840 | tf_op jit(solution)/shard_map/all_gather | solution.py:26
  7.9 693.9 %all-gather.5.cloned.1.call-start = ((), (), s32[]{:S(2)}) async-start(), calls=%async_computation.1 | async-start | bytes 8519680 | tf_op jit(solution)/shard_map/all_gather | solution.py:30
  336.5 511.4 %copy-start.1 = (f32[224,64]{0,1:T(8,128)S(1)}, f32[224,64]{0,1:T(8,128)}, u32[]{:S(2)}) copy-start(f32[224,64]{0,1:T(8,128)} %param.8) | copy-start | bytes 172036
  336.5 511.4 %copy-start.2 = (f32[224,64]{0,1:T(8,128)S(1)}, f32[224,64]{0,1:T(8,128)}, u32[]{:S(2)}) copy-start(f32[224,64]{0,1:T(8,128)} %param.9) | copy-start | bytes 172036
  336.5 511.4 %all-reduce.2.cloned.1.call-start = ((), (), s32[]{:S(2)}) async-start(), calls=%async_computation.2 | async-start | bytes 1048576 | tf_op jit(solution)/shard_map/psum | solution.py:37
Sparse Core Ops, SparseCore 0:
  10.1 322.7 all-gather.2
  336.6 365.1 all-gather.4
  709.6 138.2 all-reduce.1
where the time goes:
time: 878 us
  waiting for transfers between devices  829 us (94%)
  blocking collectives  19.5 us (2%)
  between operations  13.8 us (2%)
  matrix products  13.2 us (2%)
    all_gather x1, waiting for transfers between devices, per_device(): gathered = lax.all_gather(projected, 'mp', axis=0, tiled=True)  365 us
    all_gather x1, waiting for transfers between devices, per_device(): whole_basis = lax.all_gather(basis, 'mp', axis=0, tiled=True)  325 us
    psum x1, waiting for transfers between devices, per_device(): total_grad = lax.psum(partial_grad, 'dp')  138 us
    all_gather x1, blocking collectives, per_device(): full_direction = lax.all_gather(direction, 'dp', axis=1, tiled=True)  19.5 us
  transfers between devices with their start and end apart: 3, of which 3 were waited for; matrix products, arithmetic and copies ran while one was open for 0% of the time, Pallas kernels for 0%

commit v1 on v0

v1 whole, which is shorter than its diff:
```python
import jax
import jax.numpy as jnp
from jax import lax
from jax.experimental import pallas as pl
from jax.experimental.pallas import tpu as pltpu
from jax.sharding import PartitionSpec as P

MESH = pl.DeviceIdType.MESH
STEP = 10
beta_one = 0.9
beta_two = 0.999
epsilon = 1e-08

PARTS = 4
ORDERS = {
    0: (("z", "x", "y"), ("x", "y", "z")),
    1: (("z", "y", "x"), ("y", "x", "z")),
}
PROJ = {0: ("x", "y"), 1: ("y", "x")}
SEMS = 192


def low_high(first, second):
    lane = lax.broadcasted_iota(jnp.int32, first.shape, 1)
    low = jnp.where(lane < 64, first, pltpu.roll(second, 64, 1))
    high = jnp.where(lane < 64, pltpu.roll(first, 64, 1), second)
    return low, high


def adam(gradient, first_old, second_old):
    first_new = beta_one * first_old + (1.0 - beta_one) * gradient
    second_new = beta_two * second_old + (1.0 - beta_two) * gradient * gradient
    return first_new, second_new


def main_kernel(
    tok_hbm, grad_hbm, basis_hbm, first_hbm, second_hbm,
    dir_out, low_out, block_out,
    tok, grad, bas, first, second, bbuf, buf, acc, r1_src, r1_dst, own32, pack16, r2_dst, dbuf,
    ssem, rsem, lsem,
):
    dp, mp = lax.axis_index("dp"), lax.axis_index("mp")
    zh, core = dp // 2, dp % 2
    at = {"y": mp // 16, "z": (mp // 4) % 4, "x": mp % 4}

    def device(zh_, core_, y, z, x):
        return (zh_ * 2 + core_, y * 16 + z * 4 + x)

    def ring(dim, step):
        c = dict(at)
        zh_ = zh
        if dim == "z":
            z = (zh * 4 + at["z"] + step + 16) % 16
            zh_, c["z"] = z // 4, z % 4
        else:
            c[dim] = (at[dim] + step + 4) % 4
        return device(zh_, core, c["y"], c["z"], c["x"])

    def cube_z(step):
        return device(zh, core, at["y"], (at["z"] + step) % 4, at["x"])

    def cube(step):
        return device((zh + step) % 4, core, at["y"], at["z"], at["x"])

    sibling = device(zh, 1 - core, at["y"], at["z"], at["x"])

    count = [0]

    def fresh():
        count[0] += 1
        return count[0] - 1

    def remote(src, dst, target, index):
        return pltpu.make_async_remote_copy(
            src_ref=src, dst_ref=dst, send_sem=ssem.at[index], recv_sem=rsem.at[index],
            device_id=target, device_id_type=MESH,
        )

    loads = [
        pltpu.make_async_copy(s, d, lsem.at[i])
        for i, (s, d) in enumerate(
            ((basis_hbm, bas), (tok_hbm, tok), (grad_hbm, grad), (first_hbm, first), (second_hbm, second))
        )
    ]
    for load in loads:
        load.start()

    barrier = pltpu.get_barrier_semaphore()
    partners = [ring("x", 1), ring("x", -1), ring("x", 2), ring("y", 1), ring("y", -1), ring("y", 2)]
    partners += [ring("z", 1), ring("z", -1), ring("z", 2), ring("z", -2)]
    partners += [cube_z(1), cube_z(2), cube_z(3), cube(1), cube(2), cube(3), sibling]
    for partner in partners:
        pl.semaphore_signal(barrier, inc=1, device_id=partner, device_id_type=MESH)

    loads[0].wait()
    for a in range(2):
        t0 = bas[:, a * 256 : a * 256 + 128].astype(jnp.float32)
        t1 = bas[:, a * 256 + 128 : a * 256 + 256].astype(jnp.float32)
        low, high = low_high(t0, t1)
        own = jnp.where(core == 0, low, high).astype(jnp.bfloat16)
        bbuf[2 * a + core, at["y"], at["z"], at["x"]] = own
    pl.semaphore_wait(barrier, len(partners))

    def region(full, **other):
        return tuple(
            slice(None) if d in full else other.get(d, at[d]) for d in ("y", "z", "x")
        )

    bsem = {
        (a, r, k): fresh() for a in range(2) for r in range(2) for k in range(9)
    }
    csem = {(a, r, k): fresh() for a in range(2) for r in range(2) for k in range(4)}
    STEPS = (1, -1, 2)

    def on_cores(body):
        for c in range(2):
            pl.when(core == c)(lambda c=c: body(c))

    def basis_ref(a, c, r, idx):
        return bbuf.at[(2 * a + c, *idx, pl.ds(32 * r, 32))]

    def basis_copy(a, c, r, phase, j):
        order = ORDERS[c][r]
        ref = basis_ref(a, c, r, region(order[:phase]))
        return remote(ref, ref, ring(order[phase], STEPS[j]), bsem[a, r, phase * 3 + j])

    def sibling_copy(a, c, r, k):
        order = ORDERS[c][r]
        last = order[2]
        shift = (0, *STEPS)[k]
        ref = basis_ref(a, c, r, region(order[:2], **{last: (at[last] - shift + 4) % 4}))
        return remote(ref, ref, sibling, csem[a, r, k])

    def basis_start(a, phase):
        def body(c):
            for r in range(2):
                if phase:
                    for j in range(3):
                        basis_copy(a, c, r, phase - 1, j).wait_recv()
                for j in range(3):
                    basis_copy(a, c, r, phase, j).start()
                if phase == 2:
                    sibling_copy(a, c, r, 0).start()
        on_cores(body)

    def basis_end(a):
        def body(c):
            for r in range(2):
                for j in range(3):
                    basis_copy(a, c, r, 2, j).wait_recv()
                    sibling_copy(a, c, r, j + 1).start()
        on_cores(body)

    def basis_settle(a):
        def body(c):
            for r in range(2):
                for k in range(4):
                    sibling_copy(a, 1 - c, r, k).wait_recv()
        on_cores(body)

    def basis_drain(a):
        def body(c):
            for r in range(2):
                for phase in range(3):
                    for j in range(3):
                        basis_copy(a, c, r, phase, j).wait_send()
                for k in range(4):
                    sibling_copy(a, c, r, k).wait_send()
        on_cores(body)

    s1 = {(s, d): fresh() for s in range(PARTS) for d in (1, 2, 3)}
    s2 = {(s, j): fresh() for s in range(PARTS) for j in range(3)}
    s3 = {(s, k, e): fresh() for s in range(PARTS) for k in range(4) for e in (1, -1)}
    sf = {(s, k): fresh() for s in range(PARTS) for k in range(4)}
    SHIFT = (0, *STEPS)

    def proj_ref(s, idx):
        return buf.at[(s, *idx)]

    def copy1(s, d):
        ref = proj_ref(s, region(""))
        return remote(ref, ref, cube_z(d), s1[s, d])

    def copy2(s, j):
        ref = proj_ref(s, region("z"))
        return remote(ref, ref, ring(PROJ[s % 2][0], STEPS[j]), s2[s, j])

    def copy3(s, k, e):
        d2, d3 = PROJ[s % 2]
        ref = proj_ref(s, region("z", **{d2: (at[d2] - SHIFT[k] + 4) % 4}))
        return remote(ref, ref, ring(d3, e), s3[s, k, e])

    def forward(s, k):
        d2, d3 = PROJ[s % 2]
        e = 1 if k % 2 == 0 else -1
        ref = proj_ref(
            s, region("z", **{d2: (at[d2] - SHIFT[k] + 4) % 4, d3: (at[d3] - e + 4) % 4})
        )
        return remote(ref, ref, ring(d3, e), sf[s, k])

    def project(s):
        got = jnp.dot(
            tok[...], bbuf[s].reshape(4096, 128), preferred_element_type=jnp.float32
        )
        buf[s, at["y"], at["z"], at["x"]] = got.astype(jnp.bfloat16)
        for d in (1, 2, 3):
            copy1(s, d).start()

    def stage2(s):
        for d in (1, 2, 3):
            copy1(s, d).wait_recv()
        for j in range(3):
            copy2(s, j).start()
        for e in (1, -1):
            copy3(s, 0, e).start()

    def stage3(s):
        for j in range(3):
            copy2(s, j).wait_recv()
            for e in (1, -1):
                copy3(s, j + 1, e).start()

    def stage4(s):
        for k in range(4):
            for e in (1, -1):
                copy3(s, k, e).wait_recv()
            forward(s, k).start()

    def stage5(s):
        for k in range(4):
            forward(s, k).wait_recv()

    def multiply(s, shift, new=False):
        d3 = PROJ[s % 2][1]
        place = (at[d3] + shift + 4) % 4
        if d3 == "y":
            left = grad[:, pl.ds(pl.multiple_of(place * 2048, 2048), 2048)]
            right = buf[s, place].reshape(2048, 128)
        else:
            left = jnp.concatenate(
                [
                    grad[:, pl.ds(pl.multiple_of((j * 4 + place) * 128, 128), 128)]
                    for j in range(16)
                ],
                axis=1,
            )
            right = buf[s, :, :, place].reshape(2048, 128)
        got = jnp.dot(left, right, preferred_element_type=jnp.float32)
        if new:
            acc[s] = got
        else:
            acc[s] += got

    q1 = [fresh() for _ in range(2)]
    q2 = {(a, d): fresh() for a in range(2) for d in (1, 2, 3)}
    q3 = {d: fresh() for d in (1, 2, 3)}
    q4 = {d: fresh() for d in range(4)}

    def reduce1_copy(a):
        return remote(r1_src.at[a], r1_dst.at[a], sibling, q1[a])

    def reduce1(a):
        r1_src[a] = acc[2 * a + 1 - core]
        reduce1_copy(a).start()

    def reduce2_copy(a, d):
        return remote(pack16.at[a, (zh + d) % 4 % 2], r2_dst.at[d - 1], cube(d), q2[a, d])

    def to_half(a, d):
        return pl.when((zh + d) % 4 // 2 == a)

    def reduce2(a):
        reduce1_copy(a).wait_recv()
        total = acc[2 * a + core] + r1_dst[a]
        for b, packed in enumerate(low_high(total[:112], total[112:])):
            own32[a, b] = packed
            pack16[a, b] = packed.astype(jnp.bfloat16)
        for d in (2, 1, 3):
            to_half(a, d)(lambda d=d: reduce2_copy(a, d).start())

    def direction_copy(d):
        return remote(dbuf.at[dp], dbuf.at[dp], cube(d), q3[d])

    def pass_copy(d):
        slot = (zh - d + 4) % 4 * 2 + core
        return remote(dbuf.at[slot], dbuf.at[slot], sibling, q4[d])

    def reduce3(a):
        @pl.when(zh // 2 == a)
        def _():
            total = own32[a, zh % 2]
            for d in (1, 3, 2):
                reduce2_copy(a, d).wait_recv()
            for d in (1, 3, 2):
                total += r2_dst[d - 1].astype(jnp.float32)
            low_out[...] = total
            old = [jnp.concatenate([v[:112], v[112:]], axis=1) for v in (first[...], second[...])]
            first_new, second_new = adam(total, *old)
            corr_one = 1.0 - beta_one**STEP
            corr_two = 1.0 - beta_two**STEP
            direction = first_new / corr_one / (jnp.sqrt(second_new / corr_two) + epsilon)
            dbuf[dp] = direction.astype(jnp.bfloat16)
            for d in (2, 1, 3):
                direction_copy(d).start()
            pass_copy(0).start()

    basis_start(0, 0)
    basis_start(1, 0)
    basis_start(0, 1)
    basis_start(1, 1)
    basis_start(0, 2)
    basis_start(1, 2)
    basis_end(0)
    loads[1].wait()
    basis_settle(0)
    project(0)
    project(1)
    basis_end(1)
    stage2(0)
    stage2(1)
    basis_settle(1)
    project(2)
    project(3)
    stage3(0)
    stage3(1)
    stage2(2)
    stage2(3)
    loads[2].wait()
    multiply(0, 0, True)
    multiply(1, 0, True)
    stage4(0)
    stage4(1)
    stage3(2)
    stage3(3)
    multiply(0, 1)
    multiply(1, 1)
    multiply(0, -1)
    multiply(1, -1)
    multiply(2, 0, True)
    multiply(3, 0, True)
    block = bbuf.at[:, dp // 2, pl.ds(dp % 2 * 2, 2)]
    keep = pltpu.make_async_copy(block, block_out, lsem.at[5])
    keep.start()
    stage5(0)
    stage5(1)
    multiply(0, 2)
    multiply(1, 2)
    reduce1(0)
    stage4(2)
    stage4(3)
    reduce2(0)
    multiply(2, 1)
    multiply(3, 1)
    multiply(2, -1)
    multiply(3, -1)
    loads[3].wait()
    loads[4].wait()
    stage5(2)
    stage5(3)
    multiply(2, 2)
    multiply(3, 2)
    reduce1(1)
    reduce3(0)
    reduce2(1)
    reduce3(1)
    for d in (1, 3, 2):
        direction_copy(d).wait_recv()
        pass_copy(d).start()
    for d in (0, 1, 3, 2):
        pass_copy(d).wait_recv()
    for a in range(2):
        for c in range(2):
            pair = [dbuf[(2 * a + b) * 2 + c].astype(jnp.float32) for b in range(2)]
            top, bottom = low_high(*pair)
            columns = slice((2 * a + c) * 128, (2 * a + c + 1) * 128)
            dir_out[:112, columns] = top.astype(jnp.bfloat16)
            dir_out[112:, columns] = bottom.astype(jnp.bfloat16)

    for a in range(2):
        basis_drain(a)
    for s in range(PARTS):
        for d in (1, 2, 3):
            copy1(s, d).wait_send()
        for j in range(3):
            copy2(s, j).wait_send()
        for k in range(4):
            for e in (1, -1):
                copy3(s, k, e).wait_send()
            forward(s, k).wait_send()
    for a in range(2):
        reduce1_copy(a).wait_send()
        for d in (1, 2, 3):
            to_half(a, d)(lambda a=a, d=d: reduce2_copy(a, d).wait_send())
    for d in (1, 2, 3):
        direction_copy(d).wait_send()
    for d in range(4):
        pass_copy(d).wait_send()
    keep.wait()
    assert count[0] <= SEMS


def last_kernel(dir_ref, low_ref, block_ref, first_ref, second_ref, update, first_out, second_out):
    total = jnp.zeros((224, 512), jnp.float32)
    for s in range(PARTS):
        total += lax.dot_general(
            dir_ref[:, s * 128 : (s + 1) * 128],
            block_ref[s].reshape(512, 128),
            (((1,), (1,)), ((), ())),
            preferred_element_type=jnp.float32,
        )
    update[...] = total.astype(jnp.bfloat16)
    low = low_ref[...]
    halves = (low[:, :64], pltpu.roll(low, 64, 1)[:, :64])
    for i, gradient in enumerate(halves):
        rows = slice(112 * i, 112 * (i + 1))
        first_new, second_new = adam(gradient, first_ref[rows], second_ref[rows])
        first_out[rows] = first_new
        second_out[rows] = second_new


def per_device(tokens, grad_out, basis, first_in, second_in):
    vmem = pl.BlockSpec(memory_space=pltpu.VMEM)
    anywhere = pl.BlockSpec(memory_space=pl.ANY)
    bf16, f32 = jnp.bfloat16, jnp.float32
    direction, low, block = pl.pallas_call(
        main_kernel,
        out_shape=(
            jax.ShapeDtypeStruct((224, 512), bf16),
            jax.ShapeDtypeStruct((112, 128), f32),
            jax.ShapeDtypeStruct((4, 2, 4, 64, 128), bf16),
        ),
        in_specs=[anywhere] * 5,
        out_specs=(vmem, vmem, anywhere),
        scratch_shapes=[
            pltpu.VMEM((128, 4096), bf16),
            pltpu.VMEM((224, 8192), bf16),
            pltpu.VMEM((64, 512), bf16),
            pltpu.VMEM((224, 64), f32),
            pltpu.VMEM((224, 64), f32),
            pltpu.VMEM((PARTS, 4, 4, 4, 64, 128), bf16),
            pltpu.VMEM((PARTS, 4, 4, 4, 128, 128), bf16),
            pltpu.VMEM((PARTS, 224, 128), f32),
            pltpu.VMEM((2, 224, 128), f32),
            pltpu.VMEM((2, 224, 128), f32),
            pltpu.VMEM((2, 2, 112, 128), f32),
            pltpu.VMEM((2, 2, 112, 128), bf16),
            pltpu.VMEM((3, 112, 128), bf16),
            pltpu.VMEM((8, 112, 128), bf16),
            pltpu.SemaphoreType.DMA((SEMS,)),
            pltpu.SemaphoreType.DMA((SEMS,)),
            pltpu.SemaphoreType.DMA((6,)),
        ],
        compiler_params=pltpu.CompilerParams(
            collective_id=0, has_side_effects=True, vmem_limit_bytes=48 * 2**20
        ),
        name="gather_reduce",
    )(tokens, grad_out, basis, first_in, second_in)
    return pl.pallas_call(
        last_kernel,
        out_shape=(
            jax.ShapeDtypeStruct((224, 512), bf16),
            jax.ShapeDtypeStruct((224, 64), f32),
            jax.ShapeDtypeStruct((224, 64), f32),
        ),
        in_specs=[vmem] * 5,
        out_specs=(vmem,) * 3,
        name="update_moments",
    )(direction, low, block, first_in, second_in)


def solution(mesh):
    in_specs = (P(("dp", "mp"), None), P("mp", "dp"), P("mp", None), P("mp", "dp"), P("mp", "dp"))
    out_specs = (P("mp", "dp"), P("mp", "dp"), P("mp", "dp"))
    return jax.shard_map(
        per_device, mesh=mesh, in_specs=in_specs, out_specs=out_specs, check_vma=False
    )
```

time: 878 us -> 135 us (0.15)
  waiting for transfers between devices: 829 us -> 0 us
  Pallas kernels: 0 us -> 120 us
  blocking collectives: 19.5 us -> 0 us
  matrix products: 13.2 us -> 0 us
  between operations: 13.8 us -> 0.68 us
  local copies, waits for them, and re-layouts: 0.02 us -> 11.3 us
    all_gather x2 -> x0, waiting for transfers between devices: 690 us -> none  [the longest x1 365 us: per_device(): gathered = lax.all_gather(projected, 'mp', axis=0, tiled=True)]
    psum x1 -> x0, waiting for transfers between devices: 138 us -> none  [per_device(): total_grad = lax.psum(partial_grad, 'dp')]
    pallas_call x0 -> x2, Pallas kernels: none -> 120 us  [the longest x1 118 us: per_device(): pl.pallas_call(main_kernel, out_shape=(jax.ShapeDtypeStruct((224, 512), b...]
    all_gather x1 -> x0, blocking collectives: 19.5 us -> none  [per_device(): full_direction = lax.all_gather(direction, 'dp', axis=1, tiled=True)]
    dot_general x3 -> x0, matrix products: 13.2 us -> none  [the longest x1 7.6 us: per_device(): jnp.dot(grad_out, gathered, preferred_element_type=jnp.float32)]
  transfers between devices with their start and end apart: 3 -> 0, of which waited for: 3 -> 0; matrix products, arithmetic and copies ran while one was open for 0% -> 0% of each run, Pallas kernels for 0% -> 0%
where the time goes in v1:
time: 135 us; the launch traced here: 133 us
  Pallas kernels  120 us (89%)
  local copies, waits for them, and re-layouts  11.3 us (8%)
    pallas_call x1, Pallas kernels, per_device(): pl.pallas_call(main_kernel, out_shape=(jax.ShapeDtypeStruct((224, 512), b...  118 us
    unnamed x18, local copies, waits for them, and re-layouts  8.11 us
    pallas_call x2, local copies, waits for them, and re-layouts, per_device(): pl.pallas_call(last_kernel, out_shape=(jax.ShapeDtypeStruct((224, 512), b...  3.22 us

profile of v1, /device:TPU:1, one launch (start us, length us, event | category | flops | bytes accessed | tf_op | source)
XLA Modules:
  0.0 132.5 jit_solution(3824008982594657447)
XLA Ops:
  0.6 0.9 copy.8.first_hbm.first_ref
  1.6 0.0 copy-start.2
  1.6 1.0 copy.9.second_hbm.second_ref
  2.6 0.0 copy-start
  2.6 2.0 %copy-done = bf16[224,8192]{1,0:T(8,128)(2,1)S(1)} copy-done((bf16[224,8192]{1,0:T(8,128)(2,1)S(1)}, bf16[224,8192]{1,0:T(8,128)(2,1)}, u32[]{:S(2)}) %copy-start) | copy-done | bytes 3670040
  4.6 0.0 copy-start.1
  4.6 1.2 copy-done.1
  5.8 0.0 copy-start.6
  5.8 0.8 copy-done.6
  6.7 0.0 copy-start.3
  6.7 118.1 %gather_reduce.1 = (bf16[224,512]{1,0:T(8,128)(2,1)S(1)}, f32[112,128]{1,0:T(8,128)S(1)}, bf16[4,2,4,64,128]{4,3,2,1,0:T(8,128)(2,1)S(1)}) custom-call(bf16[128,4096]{1,0:T(8,128)(2,1)S(1)} %copy-done.1, bf16[224,8192]{1,0:T(8,128)(2,1)S(1)} %copy-done, bf16[64,512]{1,0:T(8,128)(2,1)S(1)} %copy-done.6, f32[224,64]{1,0:T(8,128)S(1)} %copy.8.first_hbm.first_ref, ...), custom_call_target="tpu_custom_call" | custom-call | tf_op jit(solution)/shard_map/gather_reduce/pallas_call | solution.py:425
  124.8 0.0 copy-start.4
  124.8 0.8 copy-done.4
  125.6 0.0 copy-start.5
  125.6 0.7 copy-done.5
  126.3 0.0 copy-start.7
  126.3 0.6 copy-done.7
  126.9 0.0 copy-done.2
  126.9 0.0 copy-done.3
  126.9 2.3 %update_moments.1 = (bf16[224,512]{1,0:T(8,128)(2,1)}, f32[224,64]{1,0:T(8,128)}, f32[224,64]{1,0:T(8,128)}) custom-call(bf16[224,512]{1,0:T(8,128)(2,1)} %copy-done.5, f32[112,128]{1,0:T(8,128)} %copy-done.7, bf16[4,2,4,64,128]{4,3,2,1,0:T(8,128)(2,1)} %copy-done.4, f32[224,64]{1,0:T(8,128)} %copy-done.2, f32[224,64]{1,0:T(8,128)} %copy-done.3), custom_call_target="tpu_custom_call" | custom-call | tf_op jit(solution)/shard_map/update_moments/pallas_call | solution.py:458
  129.3 1.6 %copy.12 = f32[224,64]{0,1:T(8,128)} copy(f32[224,64]{1,0:T(8,128)} %get-tuple-element.10) | data formatting | bytes 114688 | tf_op jit(solution)/shard_map/update_moments/pallas_call | solution.py:458
  130.9 1.6 %copy.13 = f32[224,64]{0,1:T(8,128)} copy(f32[224,64]{1,0:T(8,128)} %get-tuple-element.11) | data formatting | bytes 114688 | tf_op jit(solution)/shard_map/update_moments/pallas_call | solution.py:458
Async XLA Ops:
  1.6 125.4 %copy-start.2 = (f32[224,64]{1,0:T(8,128)}, f32[224,64]{1,0:T(8,128)S(1)}, u32[]{:S(2)}) copy-start(f32[224,64]{1,0:T(8,128)S(1)} %copy.8.first_hbm.first_ref) | copy-start | bytes 172036
  2.6 2.0 %copy-start = (bf16[224,8192]{1,0:T(8,128)(2,1)S(1)}, bf16[224,8192]{1,0:T(8,128)(2,1)}, u32[]{:S(2)}) copy-start(bf16[224,8192]{1,0:T(8,128)(2,1)} %grad_hbm.1) | copy-start | bytes 11010052
  4.6 1.2 copy-start.1
  5.8 0.8 copy-start.6
  6.7 120.3 %copy-start.3 = (f32[224,64]{1,0:T(8,128)}, f32[224,64]{1,0:T(8,128)S(1)}, u32[]{:S(2)}) copy-start(f32[224,64]{1,0:T(8,128)S(1)} %copy.9.second_hbm.second_ref) | copy-start | bytes 172036
  124.8 0.8 copy-start.4
  125.6 0.7 copy-start.5
  126.3 0.6 copy-start.7

commit v2 on v0

v2 whole, which is shorter than its diff:
```python
import jax
import jax.numpy as jnp
from jax import lax
from jax.experimental import pallas as pl
from jax.experimental.pallas import tpu as pltpu
from jax.sharding import PartitionSpec as P

MESH = pl.DeviceIdType.MESH
STEP = 10
beta_one = 0.9
beta_two = 0.999
epsilon = 1e-08

PARTS = 4
STEPS = (1, -1, 2)
SHIFT = (0, 1, -1, 2)
SPLITS = (
    (
        ((0, 32, "zxy"), (32, 16, "zyx"), (48, 16, "xyz")),
        ((0, 32, "zyx"), (32, 16, "zxy"), (48, 16, "yxz")),
    ),
    (((0, 64, "zxy"),), ((0, 64, "zyx"),)),
)
SEMS = 320


def low_high(first, second):
    lane = lax.broadcasted_iota(jnp.int32, first.shape, 1)
    low = jnp.where(lane < 64, first, pltpu.roll(second, 64, 1))
    high = jnp.where(lane < 64, pltpu.roll(first, 64, 1), second)
    return low, high


def main_kernel(
    tok_hbm, grad_hbm, basis_hbm, first_hbm, second_hbm,
    update_out, first_out, second_out,
    tok, grad, bas, first, second, bbuf, buf, turned, acc, r1_dst, own32, pack16, r2_dst, dbuf,
    ssem, rsem, lsem,
):
    dp, mp = lax.axis_index("dp"), lax.axis_index("mp")
    zh, core = dp // 2, dp % 2
    at = {"y": mp // 16, "z": (mp // 4) % 4, "x": mp % 4}

    def device(zh_, core_, y, z, x):
        return (zh_ * 2 + core_, y * 16 + z * 4 + x)

    def ring(dim, step):
        c = dict(at)
        zh_ = zh
        if dim == "z":
            z = (zh * 4 + at["z"] + step + 16) % 16
            zh_, c["z"] = z // 4, z % 4
        else:
            c[dim] = (at[dim] + step + 4) % 4
        return device(zh_, core, c["y"], c["z"], c["x"])

    def cube_z(step):
        return device(zh, core, at["y"], (at["z"] + step) % 4, at["x"])

    def cube(step):
        return device((zh + step) % 4, core, at["y"], at["z"], at["x"])

    sibling = device(zh, 1 - core, at["y"], at["z"], at["x"])

    count = [0]

    def fresh():
        count[0] += 1
        return count[0] - 1

    def remote(src, dst, target, index):
        return pltpu.make_async_remote_copy(
            src_ref=src, dst_ref=dst, send_sem=ssem.at[index], recv_sem=rsem.at[index],
            device_id=target, device_id_type=MESH,
        )

    loads = [
        pltpu.make_async_copy(s, d, lsem.at[i])
        for i, (s, d) in enumerate(
            ((basis_hbm, bas), (tok_hbm, tok), (grad_hbm, grad), (first_hbm, first), (second_hbm, second))
        )
    ]
    for load in loads:
        load.start()

    barrier = pltpu.get_barrier_semaphore()
    partners = [ring("x", 1), ring("x", -1), ring("x", 2), ring("y", 1), ring("y", -1), ring("y", 2)]
    partners += [ring("z", 1), ring("z", -1), ring("z", 2), ring("z", -2)]
    partners += [cube_z(1), cube_z(2), cube_z(3), cube(1), cube(2), cube(3), sibling]
    for partner in partners:
        pl.semaphore_signal(barrier, inc=1, device_id=partner, device_id_type=MESH)

    loads[0].wait()
    for a in range(2):
        t0 = bas[:, a * 256 : a * 256 + 128].astype(jnp.float32)
        t1 = bas[:, a * 256 + 128 : a * 256 + 256].astype(jnp.float32)
        low, high = low_high(t0, t1)
        own = jnp.where(core == 0, low, high).astype(jnp.bfloat16)
        bbuf[2 * a + core, at["y"], at["z"], at["x"]] = own
    pl.semaphore_wait(barrier, len(partners))

    def on_cores(body):
        for c in range(2):
            pl.when(core == c)(lambda c=c: body(c))

    def basis_ref(a, c, r, full, **other):
        row, rows, _ = SPLITS[a][c][r]
        idx = tuple(slice(None) if d in full else other.get(d, at[d]) for d in ("y", "z", "x"))
        return bbuf.at[(2 * a + c, *idx, pl.ds(row, rows))]

    def back(dim, k):
        return (at[dim] - SHIFT[k] + 4) % 4

    splits = {a: range(len(SPLITS[a][0])) for a in range(2)}
    b1 = {(a, r, j): fresh() for a in range(2) for r in splits[a] for j in range(3)}
    b2 = {(a, r, j): fresh() for a in range(2) for r in splits[a] for j in range(3)}
    b3 = {(a, r, k, j): fresh() for a in range(2) for r in splits[a] for k in range(4) for j in range(3)}
    bs = {(a, r, k): fresh() for a in range(2) for r in splits[a] for k in range(4)}

    def basis1(a, c, r, j):
        ref = basis_ref(a, c, r, "")
        return remote(ref, ref, ring(SPLITS[a][c][r][2][0], STEPS[j]), b1[a, r, j])

    def basis2(a, c, r, j):
        order = SPLITS[a][c][r][2]
        ref = basis_ref(a, c, r, order[0])
        return remote(ref, ref, ring(order[1], STEPS[j]), b2[a, r, j])

    def basis3(a, c, r, k, j):
        order = SPLITS[a][c][r][2]
        ref = basis_ref(a, c, r, order[0], **{order[1]: back(order[1], k)})
        return remote(ref, ref, ring(order[2], STEPS[j]), b3[a, r, k, j])

    def exchange(a, c, r, k):
        order = SPLITS[a][c][r][2]
        ref = basis_ref(a, c, r, order[:2], **{order[2]: back(order[2], k)})
        return remote(ref, ref, sibling, bs[a, r, k])

    def basis_first(a):
        def body(c):
            for r in splits[a]:
                for j in range(3):
                    basis1(a, c, r, j).start()
        on_cores(body)

    def basis_second(a):
        def body(c):
            for r in splits[a]:
                for j in range(3):
                    basis1(a, c, r, j).wait_recv()
                for j in range(3):
                    basis2(a, c, r, j).start()
                for j in range(3):
                    basis3(a, c, r, 0, j).start()
        on_cores(body)

    def basis_third(a):
        def body(c):
            for j in range(3):
                for r in splits[a]:
                    basis2(a, c, r, j).wait_recv()
                    for j_ in range(3):
                        basis3(a, c, r, j + 1, j_).start()
            for r in splits[a]:
                exchange(a, c, r, 0).start()
        on_cores(body)

    def basis_end(a):
        def body(c):
            for j in range(3):
                for r in splits[a]:
                    for k in range(4):
                        basis3(a, c, r, k, j).wait_recv()
                    exchange(a, c, r, j + 1).start()
        on_cores(body)

    def basis_settle(a):
        def body(c):
            for r in splits[a]:
                for k in range(4):
                    exchange(a, 1 - c, r, k).wait_recv()
        on_cores(body)

    def basis_drain(a):
        def body(c):
            for r in splits[a]:
                for j in range(3):
                    basis1(a, c, r, j).wait_send()
                    basis2(a, c, r, j).wait_send()
                    for k in range(4):
                        basis3(a, c, r, k, j).wait_send()
                for k in range(4):
                    exchange(a, c, r, k).wait_send()
        on_cores(body)

    def flip(i):
        return (core + i) % 2

    def part(i):
        return 2 * (i // 2) + flip(i)

    def line(i, o2=0, o3=0, z=slice(None)):
        f = flip(i)
        y = (at["y"] + f * o2 + (1 - f) * o3 + 4) % 4
        x = (at["x"] + (1 - f) * o2 + f * o3 + 4) % 4
        return buf.at[part(i), y, z, x]

    def step2(i, e):
        f = flip(i)
        return device(zh, core, (at["y"] + f * e + 4) % 4, at["z"], (at["x"] + (1 - f) * e + 4) % 4)

    def step3(i, e):
        return step2(i + 1, e)

    FINE = 2
    s1 = {(i, d): fresh() for i in range(PARTS) for d in (1, 2, 3)}
    s2 = {(i, d, e): fresh() for i in range(PARTS) for d in range(4 if i < FINE else 1) for e in (1, -1)}
    f2 = {(i, e): fresh() for i in range(PARTS) for e in (1, -1)}
    s3 = {
        (i, k, d, e): fresh()
        for i in range(PARTS)
        for k in range(4)
        for d in range(4 if i < FINE and k == 0 else 1)
        for e in (1, -1)
    }
    f3 = {(i, k): fresh() for i in range(PARTS) for k in range(4)}

    def z_back(i, d):
        return (at["z"] - d + 4) % 4 if i < FINE else slice(None)

    def copy1(i, d):
        ref = line(i, z=at["z"])
        return remote(ref, ref, cube_z(d), s1[i, d])

    def copy2(i, d, e):
        ref = line(i, z=z_back(i, d))
        return remote(ref, ref, step2(i, e), s2[i, d, e])

    def half2(i, e):
        ref = line(i, o2=-e, z=pl.ds(0 if e == 1 else 2, 2))
        return remote(ref, ref, step2(i, e), f2[i, e])

    def copy3(i, k, d, e):
        ref = line(i, o2=-SHIFT[k], z=z_back(i, d) if k == 0 else slice(None))
        return remote(ref, ref, step3(i, e), s3[i, k, d, e])

    def half3(i, k):
        e = 1 if k % 2 == 0 else -1
        ref = line(i, o2=-SHIFT[k], o3=-e)
        return remote(ref, ref, step3(i, e), f3[i, k])

    def spread(i, d):
        for e in (1, -1):
            copy2(i, d, e).start()
        for e in (1, -1):
            copy3(i, 0, d, e).start()

    def project(i):
        got = jnp.dot(
            tok[...], bbuf[part(i)].reshape(4096, 128), preferred_element_type=jnp.float32
        )
        buf[part(i), at["y"], at["z"], at["x"]] = got.astype(jnp.bfloat16)
        for d in (1, 3, 2):
            copy1(i, d).start()
        if i < FINE:
            spread(i, 0)

    def stage2(i):
        for d in (1, 3, 2):
            copy1(i, d).wait_recv()
            if i < FINE:
                spread(i, d)
        if i >= FINE:
            spread(i, 0)

    def stage3(i):
        for k, e in ((1, 1), (2, -1)):
            for d in range(4 if i < FINE else 1):
                copy2(i, d, e).wait_recv()
            half2(i, e).start()
            for e3 in (1, -1):
                copy3(i, k, 0, e3).start()

    def stage3b(i):
        for e in (1, -1):
            half2(i, e).wait_recv()
        for e3 in (1, -1):
            copy3(i, 3, 0, e3).start()

    def stage4(i):
        for k in range(4):
            for e in (1, -1):
                for d in range(4 if i < FINE and k == 0 else 1):
                    copy3(i, k, d, e).wait_recv()
            half3(i, k).start()

    def stage5(i):
        for k in range(4):
            half3(i, k).wait_recv()

    def gather_drain(i):
        for d in (1, 2, 3):
            copy1(i, d).wait_send()
        for e in (1, -1):
            half2(i, e).wait_send()
            for d in range(4 if i < FINE else 1):
                copy2(i, d, e).wait_send()
                copy3(i, 0, d, e).wait_send()
            for k in range(1, 4):
                copy3(i, k, 0, e).wait_send()
        for k in range(4):
            half3(i, k).wait_send()

    def multiply(i, shift, new=False):
        def body(f):
            place = (at["x" if f else "y"] + shift + 4) % 4
            if f == 0:
                left = grad[:, pl.ds(pl.multiple_of(place * 2048, 2048), 2048)]
                right = buf[part(i), place].reshape(2048, 128)
            else:
                left = jnp.concatenate(
                    [
                        grad[:, pl.ds(pl.multiple_of((j * 4 + place) * 128, 128), 128)]
                        for j in range(16)
                    ],
                    axis=1,
                )
                right = buf[part(i), :, :, place].reshape(2048, 128)
            got = jnp.dot(left, right, preferred_element_type=jnp.float32)
            if new:
                acc[i] = got
            else:
                acc[i] += got

        for f in range(2):
            pl.when(flip(i) == f)(lambda f=f: body(f))

    q1 = [fresh() for _ in range(2)]
    q2 = {(a, d): fresh() for a in range(2) for d in (1, 2, 3)}
    q3 = {d: fresh() for d in (1, 2, 3)}
    q4 = {d: fresh() for d in range(4)}

    def owner(step, a, body):
        pl.when((zh + step + 4) % 4 // 2 == a)(body)

    def reduce1(a):
        return remote(acc.at[2 * a + 1], r1_dst.at[a], sibling, q1[a])

    def reduce2_copy(a, d):
        return remote(pack16.at[a, (zh + d) % 4 % 2], r2_dst.at[d - 1], cube(d), q2[a, d])

    def reduce2(a):
        reduce1(a).wait_recv()
        total = (acc[2 * a] + r1_dst[a]).T
        for b in range(2):
            own32[a, b] = total[b * 64 : (b + 1) * 64]
            pack16[a, b] = total[b * 64 : (b + 1) * 64].astype(jnp.bfloat16)
        for d in (2, 1, 3):
            owner(d, a, lambda d=d: reduce2_copy(a, d).start())

    def slot(zh_, core_):
        return zh_ // 2 * 4 + core_ * 2 + zh_ % 2

    def direction_copy(d):
        ref = dbuf.at[slot(zh, core)]
        return remote(ref, ref, cube(d), q3[d])

    def pass_copy(d):
        ref = dbuf.at[slot((zh - d + 4) % 4, core)]
        return remote(ref, ref, sibling, q4[d])

    def reduce3(a):
        def body():
            total = own32[a, zh % 2]
            for d in (1, 3, 2):
                reduce2_copy(a, d).wait_recv()
            for d in (1, 3, 2):
                total += r2_dst[d - 1].astype(jnp.float32)
            first_new = beta_one * first[...] + (1.0 - beta_one) * total
            second_new = beta_two * second[...] + (1.0 - beta_two) * total * total
            corr_one = 1.0 - beta_one**STEP
            corr_two = 1.0 - beta_two**STEP
            direction = first_new / corr_one / (jnp.sqrt(second_new / corr_two) + epsilon)
            dbuf[slot(zh, core)] = direction.astype(jnp.bfloat16)
            for d in (2, 1, 3):
                direction_copy(d).start()
            pass_copy(0).start()
            first_out[...] = first_new
            second_out[...] = second_new

        owner(0, a, body)

    def pass_on(a):
        for d in (1, 3, 2):
            def body(d=d):
                direction_copy(d).wait_recv()
                pass_copy(d).start()
            owner(-d, a, body)

    def back_project(a):
        for d in (0, 1, 3, 2):
            owner(-d, a, lambda d=d: pass_copy(d).wait_recv())
        total = jnp.zeros((224, 512), jnp.float32)
        for s in (2 * a, 2 * a + 1):
            columns = jnp.concatenate([dbuf[2 * s], dbuf[2 * s + 1]], axis=0)
            columns = columns.astype(jnp.float32).T.astype(jnp.bfloat16)
            total += jnp.dot(columns, turned[s], preferred_element_type=jnp.float32)
        return total

    basis_first(0)
    basis_first(1)
    basis_second(0)
    basis_third(0)
    basis_second(1)
    basis_end(0)
    loads[1].wait()
    project(0)
    basis_third(1)
    basis_settle(0)
    project(1)
    stage2(0)
    stage2(1)
    stage3(0)
    stage3(1)
    basis_end(1)
    project(2)
    basis_settle(1)
    project(3)
    stage3b(0)
    stage3b(1)
    stage2(2)
    stage2(3)
    loads[2].wait()
    multiply(0, 0, True)
    multiply(1, 0, True)
    stage4(0)
    stage4(1)
    stage3(2)
    stage3(3)
    stage3b(2)
    stage3b(3)
    multiply(1, 1)
    multiply(1, -1)
    multiply(0, 1)
    multiply(0, -1)
    for s in range(PARTS):
        block = bbuf[s, dp // 2, pl.ds(dp % 2 * 2, 2)].reshape(512, 128)
        turned[s] = block.astype(jnp.float32).T.astype(jnp.bfloat16)
    stage5(1)
    multiply(1, 2)
    reduce1(0).start()
    stage5(0)
    multiply(0, 2)
    reduce2(0)
    multiply(2, 0, True)
    multiply(3, 0, True)
    stage4(2)
    stage4(3)
    loads[3].wait()
    loads[4].wait()
    multiply(3, 1)
    multiply(3, -1)
    multiply(2, 1)
    multiply(2, -1)
    reduce3(0)
    stage5(3)
    multiply(3, 2)
    reduce1(1).start()
    stage5(2)
    multiply(2, 2)
    reduce2(1)
    pass_on(0)
    total = back_project(0)
    reduce3(1)
    pass_on(1)
    update_out[...] = (total + back_project(1)).astype(jnp.bfloat16)

    for a in range(2):
        basis_drain(a)
    for i in range(PARTS):
        gather_drain(i)
    for a in range(2):
        reduce1(a).wait_send()
        for d in (1, 2, 3):
            owner(d, a, lambda a=a, d=d: reduce2_copy(a, d).wait_send())
    for d in (1, 2, 3):
        direction_copy(d).wait_send()
    for d in range(4):
        pass_copy(d).wait_send()
    assert count[0] <= SEMS


def last_kernel(update_in, first_in, second_in, update, first, second, sems):
    copies = [
        pltpu.make_async_copy(s, d, sems.at[i])
        for i, (s, d) in enumerate(((update_in, update), (first_in, first), (second_in, second)))
    ]
    for copy in copies:
        copy.start()
    for copy in copies:
        copy.wait()


def per_device(tokens, grad_out, basis, first_in, second_in):
    vmem = pl.BlockSpec(memory_space=pltpu.VMEM)
    hbm = pl.BlockSpec(memory_space=pltpu.HBM)
    bf16, f32 = jnp.bfloat16, jnp.float32
    results = pl.pallas_call(
        main_kernel,
        out_shape=(
            pltpu.VMEM((224, 512), bf16),
            pltpu.VMEM((64, 224), f32),
            pltpu.VMEM((64, 224), f32),
        ),
        in_specs=[hbm] * 5,
        out_specs=(vmem,) * 3,
        scratch_shapes=[
            pltpu.VMEM((128, 4096), bf16),
            pltpu.VMEM((224, 8192), bf16),
            pltpu.VMEM((64, 512), bf16),
            pltpu.VMEM((64, 224), f32),
            pltpu.VMEM((64, 224), f32),
            pltpu.VMEM((PARTS, 4, 4, 4, 64, 128), bf16),
            pltpu.VMEM((PARTS, 4, 4, 4, 128, 128), bf16),
            pltpu.VMEM((PARTS, 128, 512), bf16),
            pltpu.VMEM((PARTS, 224, 128), f32),
            pltpu.VMEM((2, 224, 128), f32),
            pltpu.VMEM((2, 2, 64, 224), f32),
            pltpu.VMEM((2, 2, 64, 224), bf16),
            pltpu.VMEM((3, 64, 224), bf16),
            pltpu.VMEM((8, 64, 224), bf16),
            pltpu.SemaphoreType.DMA((SEMS,)),
            pltpu.SemaphoreType.DMA((SEMS,)),
            pltpu.SemaphoreType.DMA((5,)),
        ],
        compiler_params=pltpu.CompilerParams(
            collective_id=0, has_side_effects=True, vmem_limit_bytes=63 * 2**20
        ),
        name="gather_reduce",
    )(tokens, grad_out, basis, first_in.T, second_in.T)
    update, first, second = pl.pallas_call(
        last_kernel,
        out_shape=(
            jax.ShapeDtypeStruct((224, 512), bf16),
            jax.ShapeDtypeStruct((64, 224), f32),
            jax.ShapeDtypeStruct((64, 224), f32),
        ),
        in_specs=[vmem] * 3,
        out_specs=(hbm,) * 3,
        scratch_shapes=[pltpu.SemaphoreType.DMA((3,))],
        name="results",
    )(*results)
    return update, first.T, second.T


def solution(mesh):
    in_specs = (P(("dp", "mp"), None), P("mp", "dp"), P("mp", None), P("mp", "dp"), P("mp", "dp"))
    out_specs = (P("mp", "dp"), P("mp", "dp"), P("mp", "dp"))
    return jax.shard_map(
        per_device, mesh=mesh, in_specs=in_specs, out_specs=out_specs, check_vma=False
    )
```

time: 878 us -> 119 us (0.14)
  the two profiles are of different devices: /device:TPU:1 before, /device:TPU:33 now
where the time goes in v2:
time: 119 us
  Pallas kernels  116 us (97%)
  local copies, waits for them, and re-layouts  1.93 us (2%)
    pallas_call x1, Pallas kernels, per_device(): pl.pallas_call(main_kernel, out_shape=(pltpu.VMEM((224, 512), bf16), pltp...  114 us

profile of v2, /device:TPU:33, one launch (start us, length us, event | category | flops | bytes accessed | tf_op | source)
XLA Modules:
  0.0 118.9 jit_solution(1519346185125309910)
XLA Ops:
  0.6 114.4 %gather_reduce.1 = (bf16[224,512]{1,0:T(8,128)(2,1)S(1)}, f32[64,224]{1,0:T(8,128)S(1)}, f32[64,224]{1,0:T(8,128)S(1)}) custom-call(bf16[128,4096]{1,0:T(8,128)(2,1)} %tok_hbm.1, bf16[224,8192]{1,0:T(8,128)(2,1)} %grad_hbm.1, bf16[64,512]{1,0:T(8,128)(2,1)} %basis_hbm.1, f32[64,224]{1,0:T(8,128)} %bitcast.4, f32[64,224]{1,0:T(8,128)} %bitcast.5), custom_call_target="tpu_custom_call" | custom-call | tf_op jit(solution)/shard_map/gather_reduce/pallas_call | solution.py:508
  115.0 0.0 copy-start
  115.1 0.7 copy-done
  115.7 0.0 copy-start.1
  115.7 0.6 copy-done.1
  116.4 0.0 copy-start.2
  116.4 0.6 copy-done.2
  117.0 1.7 %results.1 = (bf16[224,512]{1,0:T(8,128)(2,1)}, f32[64,224]{1,0:T(8,128)}, f32[64,224]{1,0:T(8,128)}) custom-call(bf16[224,512]{1,0:T(8,128)(2,1)} %copy-done, f32[64,224]{1,0:T(8,128)} %copy-done.1, f32[64,224]{1,0:T(8,128)} %copy-done.2), custom_call_target="tpu_custom_call" | custom-call | tf_op jit(solution)/shard_map/results/pallas_call | solution.py:541
Async XLA Ops:
  115.0 0.7 copy-start
  115.7 0.6 copy-start.1
  116.4 0.6 copy-start.2

commit v3 on v2

v3 whole, which is shorter than its diff:
```python
import jax
import jax.numpy as jnp
from jax import lax
from jax.experimental import pallas as pl
from jax.experimental.pallas import tpu as pltpu
from jax.sharding import PartitionSpec as P

MESH = pl.DeviceIdType.MESH
STEP = 10
beta_one = 0.9
beta_two = 0.999
epsilon = 1e-08

PARTS = 4
STEPS = (1, -1, 2)
SHIFT = (0, 1, -1, 2)
SPLITS = (
    (
        ((0, 32, "zxy"), (32, 16, "zyx"), (48, 16, "xyz")),
        ((0, 32, "zyx"), (32, 16, "zxy"), (48, 16, "yxz")),
    ),
    (
        ((0, 32, "zxy"), (32, 16, "zyx"), (48, 16, "xyz")),
        ((0, 32, "zyx"), (32, 16, "zxy"), (48, 16, "yxz")),
    ),
)
SENDS = 48
RECEIVES = 96


def low_high(first, second):
    lane = lax.broadcasted_iota(jnp.int32, first.shape, 1)
    low = jnp.where(lane < 64, first, pltpu.roll(second, 64, 1))
    high = jnp.where(lane < 64, pltpu.roll(first, 64, 1), second)
    return low, high


def main_kernel(
    tok_hbm, grad_hbm, basis_hbm, first_hbm, second_hbm,
    update_out, first_out, second_out,
    tok, grad, bas, first, second, bbuf, buf, staged, moments, turned, acc, r1_dst, own32, pack16, r2_dst, dbuf,
    ssem, rsem, lsem, hello,
):
    dp, mp = lax.axis_index("dp"), lax.axis_index("mp")
    zh, core = dp // 2, dp % 2
    at = {"y": mp // 16, "z": (mp // 4) % 4, "x": mp % 4}

    def device(zh_, core_, y, z, x):
        return (zh_ * 2 + core_, y * 16 + z * 4 + x)

    def ring(dim, step):
        c = dict(at)
        zh_ = zh
        if dim == "z":
            z = (zh * 4 + at["z"] + step + 16) % 16
            zh_, c["z"] = z // 4, z % 4
        else:
            c[dim] = (at[dim] + step + 4) % 4
        return device(zh_, core, c["y"], c["z"], c["x"])

    def cube_z(step):
        return device(zh, core, at["y"], (at["z"] + step) % 4, at["x"])

    def cube(step):
        return device((zh + step) % 4, core, at["y"], at["z"], at["x"])

    sibling = device(zh, 1 - core, at["y"], at["z"], at["x"])

    sends, receives = {}, {}

    def remote(src, dst, target, out, into):
        return pltpu.make_async_remote_copy(
            src_ref=src, dst_ref=dst,
            send_sem=ssem.at[sends.setdefault(out, len(sends))],
            recv_sem=rsem.at[receives.setdefault(into, len(receives))],
            device_id=target, device_id_type=MESH,
        )

    def sent(ref, out):
        remote(ref, ref, sibling, out, next(iter(receives))).wait_send()

    def received(ref, into):
        remote(ref, ref, sibling, next(iter(sends)), into).wait_recv()

    loads = [
        pltpu.make_async_copy(s, d, lsem.at[i])
        for i, (s, d) in enumerate(
            ((basis_hbm, bas), (tok_hbm, tok.at[core]), (grad_hbm, grad), (first_hbm, first), (second_hbm, second))
        )
    ]
    for load in loads:
        load.start()
    for i in range(PARTS):
        acc[i, 224:] = jnp.zeros((32, 128), jnp.float32)

    barrier = pltpu.get_barrier_semaphore()
    partners = [ring("x", 1), ring("x", -1), ring("x", 2), ring("y", 1), ring("y", -1), ring("y", 2)]
    partners += [ring("z", 1), ring("z", -1), ring("z", 2), ring("z", -2), sibling]
    for partner in partners:
        pl.semaphore_signal(barrier, inc=1, device_id=partner, device_id_type=MESH)

    loads[0].wait()
    for a in range(2):
        t0 = bas[:, a * 256 : a * 256 + 128].astype(jnp.float32)
        t1 = bas[:, a * 256 + 128 : a * 256 + 256].astype(jnp.float32)
        low, high = low_high(t0, t1)
        own = jnp.where(core == 0, low, high).astype(jnp.bfloat16)
        bbuf[2 * a + core, at["y"], at["z"], at["x"]] = own
    pl.semaphore_wait(barrier, len(partners))

    def greet(level):
        for step in (2 * level + 2, -2 * level - 2):
            pl.semaphore_signal(hello.at[level], inc=1, device_id=ring("z", step), device_id_type=MESH)

    def greeted(level):
        pl.semaphore_wait(hello.at[level], 2)

    greet(0)

    def tokens_copy():
        return remote(tok.at[core], tok.at[core], sibling, "tokens", "tokens")

    loads[1].wait()
    tokens_copy().start()

    def on_cores(body):
        for c in range(2):
            pl.when(core == c)(lambda c=c: body(c))

    def basis_ref(a, c, r, full, **other):
        row, rows, _ = SPLITS[a][c][r]
        idx = tuple(slice(None) if d in full else other.get(d, at[d]) for d in ("y", "z", "x"))
        return bbuf.at[(2 * a + c, *idx, pl.ds(row, rows))]

    def back(dim, k):
        return (at[dim] - SHIFT[k] + 4) % 4

    def basis1(a, c, r, j):
        ref = basis_ref(a, c, r, "")
        return remote(ref, ref, ring(SPLITS[a][c][r][2][0], STEPS[j]), ("b1", a), ("b1", a, r))

    def basis2(a, c, r, j):
        order = SPLITS[a][c][r][2]
        ref = basis_ref(a, c, r, order[0])
        return remote(ref, ref, ring(order[1], STEPS[j]), ("b2", a), ("b2", a, r, j))

    def basis3(a, c, r, k, j):
        order = SPLITS[a][c][r][2]
        ref = basis_ref(a, c, r, order[0], **{order[1]: back(order[1], k)})
        return remote(ref, ref, ring(order[2], STEPS[j]), ("b3", a), ("b3", a))

    def basis_first(a):
        def body(c):
            for r in range(3):
                for j in range(3):
                    basis1(a, c, r, j).start()
        on_cores(body)

    def basis_second(a):
        def body(c):
            for r in range(3):
                received(bbuf.at[0, 0, 0, pl.ds(0, 3), pl.ds(0, SPLITS[a][c][r][1])], ("b1", a, r))
                for j in range(3):
                    basis2(a, c, r, j).start()
                for j in range(3):
                    basis3(a, c, r, 0, j).start()
        on_cores(body)

    def basis_third(a):
        def body(c):
            for j in range(3):
                for r in range(3):
                    basis2(a, c, r, j).wait_recv()
                    for j_ in range(3):
                        basis3(a, c, r, j + 1, j_).start()
        on_cores(body)

    def basis_end(a):
        received(bbuf.at[0, pl.ds(0, 3)], ("b3", a))

    def basis_drain(a):
        sent(bbuf.at[0, 0, 0, pl.ds(0, 3)], ("b1", a))
        sent(bbuf.at[0, 0, pl.ds(0, 3)], ("b2", a))
        sent(bbuf.at[0, pl.ds(0, 3)], ("b3", a))

    def block_copy(a):
        other = zh * 2 + 1 - core
        ref = bbuf.at[2 * a + core, other // 2, pl.ds(other % 2 * 2, 2)]
        return remote(ref, ref, sibling, ("block", a), ("block", a))

    def flip(i):
        return (core + i) % 2

    def part(i):
        return 2 * (i // 2) + flip(i)

    def line(i, o2=0, o3=0, z=slice(None)):
        f = flip(i)
        y = (at["y"] + f * o2 + (1 - f) * o3 + 4) % 4
        x = (at["x"] + (1 - f) * o2 + f * o3 + 4) % 4
        return buf.at[part(i), y, z, x]

    def step2(i, e):
        f = flip(i)
        return device(zh, core, (at["y"] + f * e + 4) % 4, at["z"], (at["x"] + (1 - f) * e + 4) % 4)

    def step3(i, e):
        return step2(i + 1, e)

    FINE = 2

    def z_back(i, d):
        return (at["z"] - d + 4) % 4 if i < FINE else slice(None)

    def copy1(i, d):
        ref = line(i, z=at["z"])
        return remote(ref, ref, cube_z(d), ("s1", i), ("s1", i, d if i < FINE else 0))

    def copy2(i, d, e):
        ref = line(i, z=z_back(i, d))
        return remote(ref, ref, step2(i, e), ("s2", i), ("s2", i, e))

    def half2(i, e):
        ref = line(i, o2=-e, z=pl.ds(0 if e == 1 else 2, 2))
        return remote(ref, ref, step2(i, e), ("s2", i), ("f2", i))

    def copy3(i, k, d, e):
        ref = line(i, o2=-SHIFT[k], z=z_back(i, d) if k == 0 else slice(None))
        return remote(ref, ref, step3(i, e), ("s3", i), ("s3", i, k))

    def half3(i, k):
        e = 1 if k % 2 == 0 else -1
        ref = line(i, o2=-SHIFT[k], o3=-e)
        return remote(ref, ref, step3(i, e), ("s3", i), ("f3", i))

    def spread(i, d):
        for e in (1, -1):
            copy2(i, d, e).start()
        for e in (1, -1):
            copy3(i, 0, d, e).start()

    def place(i):
        return buf.at[part(i), at["y"], at["z"], at["x"]]

    def result_copy(a):
        return remote(staged.at[a], place(2 * a), sibling, ("result", a), ("result", a))

    def begin(i):
        for d in (1, 3, 2):
            copy1(i, d).start()
        if i < FINE:
            spread(i, 0)

    def project(a):
        got = jnp.dot(
            tok[...].reshape(256, 4096),
            bbuf[2 * a + core].reshape(4096, 128),
            preferred_element_type=jnp.float32,
        )
        got = got.astype(jnp.bfloat16)
        staged[a] = jnp.where(core == 0, got[128:], got[:128])
        result_copy(a).start()
        buf[2 * a + core, at["y"], at["z"], at["x"]] = jnp.where(core == 0, got[:128], got[128:])
        begin(2 * a)

    def adopt(a):
        result_copy(a).wait_recv()
        begin(2 * a + 1)

    def stage2(i):
        if i < FINE:
            for d in (1, 3, 2):
                copy1(i, d).wait_recv()
                spread(i, d)
        else:
            received(buf.at[0, 0, 0, pl.ds(0, 3)], ("s1", i, 0))
            spread(i, 0)

    def stage3(i):
        for k, e in ((1, 1), (2, -1)):
            received(buf.at[0, 0, 0], ("s2", i, e))
            half2(i, e).start()
            for e3 in (1, -1):
                copy3(i, k, 0, e3).start()

    def stage3b(i):
        received(buf.at[0, 0, 0], ("f2", i))
        for e3 in (1, -1):
            copy3(i, 3, 0, e3).start()

    def stage4(i, which=(0, 1, 2, 3)):
        for k in which:
            received(buf.at[0, 0, pl.ds(0, 2)], ("s3", i, k))
            half3(i, k).start()

    def stage5(i):
        received(buf.at[0, 0], ("f3", i))

    def gather_drain(i):
        sent(buf.at[0, 0, 0, pl.ds(0, 3)], ("s1", i))
        sent(buf.at[0, 0, pl.ds(0, 3)], ("s2", i))
        sent(buf.at[0, pl.ds(0, 3)], ("s3", i))

    def multiply(i, shift, new=False):
        def body(f):
            place = (at["x" if f else "y"] + shift + 4) % 4
            if f == 0:
                left = grad[:, pl.ds(pl.multiple_of(place * 2048, 2048), 2048)]
                right = buf[part(i), place].reshape(2048, 128)
            else:
                left = jnp.concatenate(
                    [
                        grad[:, pl.ds(pl.multiple_of((j * 4 + place) * 128, 128), 128)]
                        for j in range(16)
                    ],
                    axis=1,
                )
                right = buf[part(i), :, :, place].reshape(2048, 128)
            got = jnp.dot(left, right, preferred_element_type=jnp.float32)
            if new:
                acc[i, :224] = got
            else:
                acc[i, :224] += got

        for f in range(2):
            pl.when(flip(i) == f)(lambda f=f: body(f))

    def owner(step, a, body):
        pl.when((zh + step + 4) % 4 // 2 == a)(body)

    def reduce1(a):
        return remote(acc.at[2 * a + 1], r1_dst.at[a], sibling, ("q1", a), ("q1", a))

    def reduce2_copy(a, d):
        return remote(pack16.at[a, (zh + d) % 4 % 2], r2_dst.at[d - 1], cube(d), ("q2", a, d), ("q2", a, d))

    def reduce2(a):
        reduce1(a).wait_recv()
        total = (acc[2 * a] + r1_dst[a]).T
        for b in range(2):
            own32[a, b] = total[b * 64 : (b + 1) * 64]
            pack16[a, b] = total[b * 64 : (b + 1) * 64].astype(jnp.bfloat16)
        for d in (2, 1, 3):
            owner(d, a, lambda d=d: reduce2_copy(a, d).start())

    def slot(zh_, core_):
        return zh_ // 2 * 4 + core_ * 2 + zh_ % 2

    def direction_copy(d):
        ref = dbuf.at[slot(zh, core)]
        return remote(ref, ref, cube(d), ("q3", d), ("q3", d))

    def pass_copy(d):
        ref = dbuf.at[slot((zh - d + 4) % 4, core)]
        return remote(ref, ref, sibling, ("q4", d), ("q4", d))

    keep = [
        pltpu.make_async_copy(moments.at[n], out, lsem.at[5 + n])
        for n, out in enumerate((first_out, second_out))
    ]

    def reduce3(a):
        def body():
            total = own32[a, zh % 2][:, :224]
            for d in (1, 3, 2):
                reduce2_copy(a, d).wait_recv()
            for d in (1, 3, 2):
                total += r2_dst[d - 1][:, :224].astype(jnp.float32)
            first_new = beta_one * first[...] + (1.0 - beta_one) * total
            second_new = beta_two * second[...] + (1.0 - beta_two) * total * total
            corr_one = 1.0 - beta_one**STEP
            corr_two = 1.0 - beta_two**STEP
            direction = first_new / corr_one / (jnp.sqrt(second_new / corr_two) + epsilon)
            mine = slot(zh, core)
            dbuf[mine, :, 128:] = jnp.zeros((64, 128), jnp.bfloat16)
            dbuf[mine, :, :224] = direction.astype(jnp.bfloat16)
            for d in (2, 1, 3):
                direction_copy(d).start()
            pass_copy(0).start()
            moments[0] = first_new
            moments[1] = second_new
            for copy in keep:
                copy.start()

        owner(0, a, body)

    def pass_on(a):
        for d in (1, 3, 2):
            def body(d=d):
                direction_copy(d).wait_recv()
                pass_copy(d).start()
            owner(-d, a, body)

    def back_project(a):
        for d in (0, 1, 3, 2):
            owner(-d, a, lambda d=d: pass_copy(d).wait_recv())
        total = jnp.zeros((256, 512), jnp.float32)
        for s in (2 * a, 2 * a + 1):
            columns = jnp.concatenate([dbuf[2 * s], dbuf[2 * s + 1]], axis=0)
            columns = columns.astype(jnp.float32).T.astype(jnp.bfloat16)
            total += jnp.dot(columns, turned[s], preferred_element_type=jnp.float32)
        return total

    basis_first(0)
    basis_first(1)
    basis_second(0)
    basis_third(0)
    basis_second(1)
    greeted(0)
    greet(1)
    tokens_copy().wait_recv()
    basis_end(0)
    project(0)
    basis_third(1)
    adopt(0)
    stage2(0)
    stage2(1)
    basis_end(1)
    project(1)
    adopt(1)
    for a in range(2):
        block_copy(a).start()
    stage3(0)
    stage3(1)
    stage4(0, (0,))
    stage4(1, (0,))
    stage2(2)
    stage2(3)
    stage3b(0)
    stage3b(1)
    stage4(0, (1, 2))
    stage4(1, (1, 2))
    greeted(1)
    loads[2].wait()
    multiply(0, 0, True)
    multiply(1, 0, True)
    stage3(2)
    stage3(3)
    stage4(0, (3,))
    stage4(1, (3,))
    stage3b(2)
    stage3b(3)
    stage4(2, (0,))
    stage4(3, (0,))
    multiply(1, 1)
    multiply(1, -1)
    multiply(0, 1)
    multiply(0, -1)
    stage5(1)
    multiply(1, 2)
    reduce1(0).start()
    stage5(0)
    multiply(0, 2)
    stage4(2, (1,))
    stage4(3, (1,))
    reduce2(0)
    multiply(2, 0, True)
    multiply(3, 0, True)
    stage4(2, (2,))
    stage4(3, (2,))
    for a in range(2):
        block_copy(a).wait_recv()
    for s in range(PARTS):
        block = bbuf[s, dp // 2, pl.ds(dp % 2 * 2, 2)].reshape(512, 128)
        turned[s] = block.astype(jnp.float32).T.astype(jnp.bfloat16)
    loads[3].wait()
    loads[4].wait()
    stage4(2, (3,))
    stage4(3, (3,))
    reduce3(0)
    multiply(3, 1)
    multiply(3, -1)
    multiply(2, 1)
    multiply(2, -1)
    stage5(3)
    multiply(3, 2)
    reduce1(1).start()
    stage5(2)
    multiply(2, 2)
    reduce2(1)
    reduce3(1)
    pass_on(0)
    total = back_project(0)
    pass_on(1)
    update_out[...] = (total + back_project(1))[:224].astype(jnp.bfloat16)

    tokens_copy().wait_send()
    for a in range(2):
        basis_drain(a)
        result_copy(a).wait_send()
        block_copy(a).wait_send()
    for i in range(PARTS):
        gather_drain(i)
    for a in range(2):
        reduce1(a).wait_send()
        for d in (1, 2, 3):
            owner(d, a, lambda a=a, d=d: reduce2_copy(a, d).wait_send())
    for d in (1, 2, 3):
        direction_copy(d).wait_send()
    for d in range(4):
        pass_copy(d).wait_send()
    for copy in keep:
        copy.wait()
    assert len(sends) <= SENDS and len(receives) <= RECEIVES


def last_kernel(update_in, first_in, second_in, update, first, second, *scratch):
    held, sems = scratch[:3], scratch[3]
    ins, outs = (update_in, first_in, second_in), (update, first, second)
    loads = [pltpu.make_async_copy(s, d, sems.at[i]) for i, (s, d) in enumerate(zip(ins, held))]
    stores = [pltpu.make_async_copy(s, d, sems.at[3 + i]) for i, (s, d) in enumerate(zip(held, outs))]
    for load in loads:
        load.start()
    for load, store in zip(loads, stores):
        load.wait()
        store.start()
    for store in stores:
        store.wait()


def per_device(tokens, grad_out, basis, first_in, second_in):
    vmem = pl.BlockSpec(memory_space=pltpu.VMEM)
    hbm = pl.BlockSpec(memory_space=pltpu.HBM)
    bf16, f32 = jnp.bfloat16, jnp.float32
    outs = (
        jax.ShapeDtypeStruct((224, 512), bf16),
        jax.ShapeDtypeStruct((64, 224), f32),
        jax.ShapeDtypeStruct((64, 224), f32),
    )
    results = pl.pallas_call(
        main_kernel,
        out_shape=outs,
        in_specs=[hbm] * 5,
        out_specs=(vmem, hbm, hbm),
        scratch_shapes=[
            pltpu.VMEM((2, 128, 4096), bf16),
            pltpu.VMEM((224, 8192), bf16),
            pltpu.VMEM((64, 512), bf16),
            pltpu.VMEM((64, 224), f32),
            pltpu.VMEM((64, 224), f32),
            pltpu.VMEM((PARTS, 4, 4, 4, 64, 128), bf16),
            pltpu.VMEM((PARTS, 4, 4, 4, 128, 128), bf16),
            pltpu.VMEM((2, 128, 128), bf16),
            pltpu.VMEM((2, 64, 224), f32),
            pltpu.VMEM((PARTS, 128, 512), bf16),
            pltpu.VMEM((PARTS, 256, 128), f32),
            pltpu.VMEM((2, 256, 128), f32),
            pltpu.VMEM((2, 2, 64, 256), f32),
            pltpu.VMEM((2, 2, 64, 256), bf16),
            pltpu.VMEM((3, 64, 256), bf16),
            pltpu.VMEM((8, 64, 256), bf16),
            pltpu.SemaphoreType.DMA((SENDS,)),
            pltpu.SemaphoreType.DMA((RECEIVES,)),
            pltpu.SemaphoreType.DMA((7,)),
            pltpu.SemaphoreType.REGULAR((2,)),
        ],
        compiler_params=pltpu.CompilerParams(
            collective_id=0, has_side_effects=True, vmem_limit_bytes=66_600_000
        ),
        name="gather_reduce",
    )(tokens, grad_out, basis, first_in.T, second_in.T)
    update, first, second = pl.pallas_call(
        last_kernel,
        out_shape=outs,
        in_specs=[hbm] * 3,
        out_specs=(hbm,) * 3,
        scratch_shapes=[pltpu.VMEM(o.shape, o.dtype) for o in outs] + [pltpu.SemaphoreType.DMA((6,))],
        compiler_params=pltpu.CompilerParams(vmem_limit_bytes=66_600_000),
        name="results",
    )(*results)
    return update, first.T, second.T


def solution(mesh):
    in_specs = (P(("dp", "mp"), None), P("mp", "dp"), P("mp", None), P("mp", "dp"), P("mp", "dp"))
    out_specs = (P("mp", "dp"), P("mp", "dp"), P("mp", "dp"))
    return jax.shard_map(
        per_device, mesh=mesh, in_specs=in_specs, out_specs=out_specs, check_vma=False
    )
```

time: 119 us -> 111 us (0.933)
  the two profiles are of different devices: /device:TPU:33 before, /device:TPU:1 now
where the time goes in v3:
time: 111 us; the launch traced here: 110 us
  Pallas kernels  109 us (98%)
    pallas_call x1, Pallas kernels, per_device(): pl.pallas_call(main_kernel, out_shape=outs, in_specs=[hbm] * 5, out_specs...  107 us

profile of v3, /device:TPU:1, one launch (start us, length us, event | category | flops | bytes accessed | tf_op | source)
XLA Modules:
  0.0 109.6 jit_solution(5497659316710792950)
XLA Ops:
  0.6 107.1 %gather_reduce.1 = (bf16[224,512]{1,0:T(8,128)(2,1)}, f32[64,224]{1,0:T(8,128)}, f32[64,224]{1,0:T(8,128)}) custom-call(bf16[128,4096]{1,0:T(8,128)(2,1)} %tok_hbm.1, bf16[224,8192]{1,0:T(8,128)(2,1)} %grad_hbm.1, bf16[64,512]{1,0:T(8,128)(2,1)} %basis_hbm.1, f32[64,224]{1,0:T(8,128)} %bitcast.4, f32[64,224]{1,0:T(8,128)} %bitcast.5), custom_call_target="tpu_custom_call" | custom-call | tf_op jit(solution)/shard_map/gather_reduce/pallas_call | solution.py:530
  107.7 1.7 %results.1 = (bf16[224,512]{1,0:T(8,128)(2,1)}, f32[64,224]{1,0:T(8,128)}, f32[64,224]{1,0:T(8,128)}) custom-call(bf16[224,512]{1,0:T(8,128)(2,1)} %get-tuple-element.9.update_in, f32[64,224]{1,0:T(8,128)} %get-tuple-element.10.first_in, f32[64,224]{1,0:T(8,128)} %get-tuple-element.11.second_in), custom_call_target="tpu_custom_call" | custom-call | tf_op jit(solution)/shard_map/results/pallas_call | solution.py:562

commit v4 on v3

--- a/solution.py
+++ b/solution.py
@@ -24,8 +24,9 @@
         ((0, 32, "zyx"), (32, 16, "zxy"), (48, 16, "yxz")),
     ),
 )
-SENDS = 48
-RECEIVES = 96
+ROWS = (112, 112)
+SENDS = 50
+RECEIVES = 98
 
 
 def low_high(first, second):
@@ -120,9 +121,6 @@
     def tokens_copy():
         return remote(tok.at[core], tok.at[core], sibling, "tokens", "tokens")
 
-    loads[1].wait()
-    tokens_copy().start()
-
     def on_cores(body):
         for c in range(2):
             pl.when(core == c)(lambda c=c: body(c))
@@ -194,11 +192,17 @@
     def part(i):
         return 2 * (i // 2) + flip(i)
 
-    def line(i, o2=0, o3=0, z=slice(None)):
+    def rows_of(i):
+        return pl.ds(0, ROWS[i // 2])
+
+    def rest_of(i):
+        return pl.ds(ROWS[i // 2], 128 - ROWS[i // 2])
+
+    def line(i, o2=0, o3=0, z=slice(None), rows=None):
         f = flip(i)
         y = (at["y"] + f * o2 + (1 - f) * o3 + 4) % 4
         x = (at["x"] + (1 - f) * o2 + f * o3 + 4) % 4
-        return buf.at[part(i), y, z, x]
+        return buf.at[part(i), y, z, x, rows_of(i) if rows is None else rows]
 
     def step2(i, e):
         f = flip(i)
@@ -232,6 +236,34 @@
         e = 1 if k % 2 == 0 else -1
         ref = line(i, o2=-SHIFT[k], o3=-e)
         return remote(ref, ref, step3(i, e), ("s3", i), ("f3", i))
+
+    def rest1(i, j):
+        ref = line(i, z=at["z"], rows=rest_of(i))
+        return remote(ref, ref, step2(i, STEPS[j]), ("p1", i), ("p1", i))
+
+    def rest2(i, k, j):
+        ref = line(i, o2=-SHIFT[k], z=at["z"], rows=rest_of(i))
+        return remote(ref, ref, step3(i, STEPS[j]), ("p2", i), ("p2", i))
+
+    def rest3(i, d):
+        ref = buf.at[part(i), :, at["z"], :, rest_of(i)]
+        return remote(ref, ref, cube_z(d), ("p3", i), ("p3", i))
+
+    def rest_second(i):
+        for j in range(3):
+            rest2(i, 0, j).start()
+        received(buf.at[0, 0, 0, pl.ds(0, 3), rest_of(i)], ("p1", i))
+        for k in range(1, 4):
+            for j in range(3):
+                rest2(i, k, j).start()
+
+    def rest_third(i):
+        received(buf.at[0, 0, pl.ds(0, 3), :, rest_of(i)], ("p2", i))
+        for d in (1, 3, 2):
+            rest3(i, d).start()
+
+    def rest_end(i):
+        received(buf.at[0, pl.ds(0, 3), :, :, rest_of(i)], ("p3", i))
 
     def spread(i, d):
         for e in (1, -1):
@@ -250,6 +282,8 @@
             copy1(i, d).start()
         if i < FINE:
             spread(i, 0)
+        for j in range(3):
+            rest1(i, j).start()
 
     def project(a):
         got = jnp.dot(
@@ -273,33 +307,36 @@
                 copy1(i, d).wait_recv()
                 spread(i, d)
         else:
-            received(buf.at[0, 0, 0, pl.ds(0, 3)], ("s1", i, 0))
+            received(buf.at[0, 0, 0, pl.ds(0, 3), rows_of(i)], ("s1", i, 0))
             spread(i, 0)
 
     def stage3(i):
         for k, e in ((1, 1), (2, -1)):
-            received(buf.at[0, 0, 0], ("s2", i, e))
+            received(buf.at[0, 0, 0, :, rows_of(i)], ("s2", i, e))
             half2(i, e).start()
             for e3 in (1, -1):
                 copy3(i, k, 0, e3).start()
 
     def stage3b(i):
-        received(buf.at[0, 0, 0], ("f2", i))
+        received(buf.at[0, 0, 0, :, rows_of(i)], ("f2", i))
         for e3 in (1, -1):
             copy3(i, 3, 0, e3).start()
 
     def stage4(i, which=(0, 1, 2, 3)):
         for k in which:
-            received(buf.at[0, 0, pl.ds(0, 2)], ("s3", i, k))
+            received(buf.at[0, 0, pl.ds(0, 2), :, rows_of(i)], ("s3", i, k))
             half3(i, k).start()
 
     def stage5(i):
-        received(buf.at[0, 0], ("f3", i))
+        received(buf.at[0, 0, :, :, rows_of(i)], ("f3", i))
 
     def gather_drain(i):
-        sent(buf.at[0, 0, 0, pl.ds(0, 3)], ("s1", i))
-        sent(buf.at[0, 0, pl.ds(0, 3)], ("s2", i))
-        sent(buf.at[0, pl.ds(0, 3)], ("s3", i))
+        sent(buf.at[0, 0, 0, pl.ds(0, 3), rows_of(i)], ("s1", i))
+        sent(buf.at[0, 0, pl.ds(0, 3), :, rows_of(i)], ("s2", i))
+        sent(buf.at[0, pl.ds(0, 3), :, :, rows_of(i)], ("s3", i))
+        sent(buf.at[0, 0, 0, pl.ds(0, 3), rest_of(i)], ("p1", i))
+        sent(buf.at[0, 0, pl.ds(0, 3), :, rest_of(i)], ("p2", i))
+        sent(buf.at[0, pl.ds(0, 3), :, :, rest_of(i)], ("p3", i))
 
     def multiply(i, shift, new=False):
         def body(f):
@@ -403,6 +440,8 @@
 
     basis_first(0)
     basis_first(1)
+    loads[1].wait()
+    tokens_copy().start()
     basis_second(0)
     basis_third(0)
     basis_second(1)
@@ -414,50 +453,62 @@
     basis_third(1)
     adopt(0)
     stage2(0)
-    stage2(1)
     basis_end(1)
     project(1)
+    stage2(1)
+    rest_second(0)
+    rest_second(1)
     adopt(1)
     for a in range(2):
         block_copy(a).start()
     stage3(0)
     stage3(1)
+    rest_third(0)
+    rest_third(1)
+    rest_second(2)
+    rest_second(3)
     stage4(0, (0,))
     stage4(1, (0,))
     stage2(2)
     stage2(3)
     stage3b(0)
     stage3b(1)
+    rest_third(2)
+    rest_third(3)
     stage4(0, (1, 2))
     stage4(1, (1, 2))
     greeted(1)
     loads[2].wait()
-    multiply(0, 0, True)
-    multiply(1, 0, True)
     stage3(2)
     stage3(3)
+    stage4(2, (0,))
+    stage4(3, (0,))
     stage4(0, (3,))
     stage4(1, (3,))
+    rest_end(1)
+    multiply(1, 0, True)
+    multiply(1, 1)
+    multiply(1, -1)
     stage3b(2)
     stage3b(3)
-    stage4(2, (0,))
-    stage4(3, (0,))
-    multiply(1, 1)
-    multiply(1, -1)
+    rest_end(0)
+    multiply(0, 0, True)
     multiply(0, 1)
     multiply(0, -1)
+    stage4(2, (1, 2))
+    stage4(3, (1, 2))
     stage5(1)
     multiply(1, 2)
     reduce1(0).start()
     stage5(0)
     multiply(0, 2)
-    stage4(2, (1,))
-    stage4(3, (1,))
     reduce2(0)
+    rest_end(2)
     multiply(2, 0, True)
+    stage4(2, (3,))
+    stage4(3, (3,))
+    rest_end(3)
     multiply(3, 0, True)
-    stage4(2, (2,))
-    stage4(3, (2,))
     for a in range(2):
         block_copy(a).wait_recv()
     for s in range(PARTS):
@@ -465,9 +516,6 @@
         turned[s] = block.astype(jnp.float32).T.astype(jnp.bfloat16)
     loads[3].wait()
     loads[4].wait()
-    stage4(2, (3,))
-    stage4(3, (3,))
-    reduce3(0)
     multiply(3, 1)
     multiply(3, -1)
     multiply(2, 1)
@@ -478,6 +526,7 @@
     stage5(2)
     multiply(2, 2)
     reduce2(1)
+    reduce3(0)
     reduce3(1)
     pass_on(0)
     total = back_project(0)

time: 111 us -> 103 us (0.928); the launches traced: 110 us -> 103 us
  Pallas kernels: 109 us -> 102 us
    pallas_call x1, Pallas kernels: 107 us -> 101 us  [per_device(): pl.pallas_call(main_kernel, out_shape=outs, in_specs=[hbm] * 5, out_specs...]
where the time goes in v4:
time: 103 us
  Pallas kernels  102 us (99%)
    pallas_call x1, Pallas kernels, per_device(): pl.pallas_call(main_kernel, out_shape=outs, in_specs=[hbm] * 5, out_specs...  101 us

profile of v4, /device:TPU:1, one launch (start us, length us, event | category | flops | bytes accessed | tf_op | source)
XLA Modules:
  0.0 103.2 jit_solution(494649850508649957)
XLA Ops:
  0.6 100.7 %gather_reduce.1 = (bf16[224,512]{1,0:T(8,128)(2,1)}, f32[64,224]{1,0:T(8,128)}, f32[64,224]{1,0:T(8,128)}) custom-call(bf16[128,4096]{1,0:T(8,128)(2,1)} %tok_hbm.1, bf16[224,8192]{1,0:T(8,128)(2,1)} %grad_hbm.1, bf16[64,512]{1,0:T(8,128)(2,1)} %basis_hbm.1, f32[64,224]{1,0:T(8,128)} %bitcast.4, f32[64,224]{1,0:T(8,128)} %bitcast.5), custom_call_target="tpu_custom_call" | custom-call | tf_op jit(solution)/shard_map/gather_reduce/pallas_call | solution.py:579
  101.3 1.7 %results.1 = (bf16[224,512]{1,0:T(8,128)(2,1)}, f32[64,224]{1,0:T(8,128)}, f32[64,224]{1,0:T(8,128)}) custom-call(bf16[224,512]{1,0:T(8,128)(2,1)} %get-tuple-element.9.update_in, f32[64,224]{1,0:T(8,128)} %get-tuple-element.10.first_in, f32[64,224]{1,0:T(8,128)} %get-tuple-element.11.second_in), custom_call_target="tpu_custom_call" | custom-call | tf_op jit(solution)/shard_map/results/pallas_call | solution.py:611

commit v5 on v4

--- a/solution.py
+++ b/solution.py
@@ -160,6 +160,7 @@
                 received(bbuf.at[0, 0, 0, pl.ds(0, 3), pl.ds(0, SPLITS[a][c][r][1])], ("b1", a, r))
                 for j in range(3):
                     basis2(a, c, r, j).start()
+            for r in range(3):
                 for j in range(3):
                     basis3(a, c, r, 0, j).start()
         on_cores(body)
@@ -490,11 +491,11 @@
     multiply(1, 1)
     multiply(1, -1)
     stage3b(2)
-    stage3b(3)
     rest_end(0)
     multiply(0, 0, True)
     multiply(0, 1)
     multiply(0, -1)
+    stage3b(3)
     stage4(2, (1, 2))
     stage4(3, (1, 2))
     stage5(1)

time: 103 us -> 103 us (level); the launches traced: 103 us -> 102 us
    pallas_call x1, Pallas kernels: 101 us -> 99.7 us  [per_device(): pl.pallas_call(main_kernel, out_shape=outs, in_specs=[hbm] * 5, out_specs...]
where the time goes in v5:
time: 103 us; the launch traced here: 102 us
  Pallas kernels  101 us (98%)
    pallas_call x1, Pallas kernels, per_device(): pl.pallas_call(main_kernel, out_shape=outs, in_specs=[hbm] * 5, out_specs...  99.7 us

profile of v5, /device:TPU:1, one launch (start us, length us, event | category | flops | bytes accessed | tf_op | source)
XLA Modules:
  0.0 102.2 jit_solution(2546467189459436802)
XLA Ops:
  0.6 99.7 %gather_reduce.1 = (bf16[224,512]{1,0:T(8,128)(2,1)}, f32[64,224]{1,0:T(8,128)}, f32[64,224]{1,0:T(8,128)}) custom-call(bf16[128,4096]{1,0:T(8,128)(2,1)} %tok_hbm.1, bf16[224,8192]{1,0:T(8,128)(2,1)} %grad_hbm.1, bf16[64,512]{1,0:T(8,128)(2,1)} %basis_hbm.1, f32[64,224]{1,0:T(8,128)} %bitcast.4, f32[64,224]{1,0:T(8,128)} %bitcast.5), custom_call_target="tpu_custom_call" | custom-call | tf_op jit(solution)/shard_map/gather_reduce/pallas_call | solution.py:580
  100.3 1.7 %results.1 = (bf16[224,512]{1,0:T(8,128)(2,1)}, f32[64,224]{1,0:T(8,128)}, f32[64,224]{1,0:T(8,128)}) custom-call(bf16[224,512]{1,0:T(8,128)(2,1)} %get-tuple-element.9.update_in, f32[64,224]{1,0:T(8,128)} %get-tuple-element.10.first_in, f32[64,224]{1,0:T(8,128)} %get-tuple-element.11.second_in), custom_call_target="tpu_custom_call" | custom-call | tf_op jit(solution)/shard_map/results/pallas_call | solution.py:612
